TPU v7x, 32 devices: a whole 2x2x4 slice. The times are simulated.
32 devices in a mesh: lat: 8 (over z, x), lev: 4 (over y, core).
Axes of the slice: x: 2, y: 2, z: 4, core: 2. Of those that a mesh axis runs over, the one named last changes fastest.
Arguments:
- particle_mass_fraction: float32 [20, 64, 8, 360], P(None, 'lat', 'lev'), may hold values from 0.1 to 2
- meridional_cfl_factor: float32 [64, 8, 360], P('lat', 'lev'), may hold values from -0.45 to 0.45
- thermal_state_kelvins: float32 [64, 8, 360], P('lat', 'lev'), may hold values from 200 to 300
- logarithmic_barometric_span: float32 [8], P('lev'), may hold values from 0.06 to 0.2
- gravitational_fall_kilometres: float32 [20], replicated, may hold values from 0.02 to 20
- zonal_cfl_factor: float32 [64, 8, 360], P('lat', None, 'lev'), may hold values from -0.45 to 0.45
- collision_rate_matrix: float32 [20, 20], replicated, may hold values from 0.02 to 0.2
Outputs:
- dust_out: float32 [20, 64, 8, 360], P(None, 'lat', None, 'lev')
- height: float32 [64, 8, 360], P('lat', 'lev')
All inputs are finite; a program needn't handle non-finite values.
Results may differ from a plain program's by a relative error of at most 0.000067.
Values sent between devices are 32-bit elements; how exact they have to be, the bound alone decides.
A program may use at most 128 MiB of HBM per device.

v0:
```python
import jax
import jax.numpy as jnp
from jax import lax
from jax.sharding import PartitionSpec as P

specific_air_factor = 0.0293
scale_height = 7.0


def extended_2(x, sides, width, wrap):
    for axis, dim in sides:
        peers, length = (lax.axis_size(axis), x.shape[dim])
        up = [(i, (i + 1) % peers) for i in range(peers if wrap else peers - 1)]
        down = [(j, i) for i, j in up]
        last = lax.slice_in_dim(x, length - width, length, axis=dim)
        leading = lax.slice_in_dim(x, 0, width, axis=dim)
        before = lax.ppermute(last, axis, up)
        after = lax.ppermute(leading, axis, down)
        x = jnp.concatenate([before, x, after], axis=dim)
    return x


def prefix(value, axis, join, neutral):
    count, mine = (lax.axis_size(axis), lax.axis_index(axis))
    pieces = lax.all_gather(value, axis)
    pieces = pieces[::-1]
    mine = count - 1 - mine
    subtotal = jnp.full_like(value, 0) + jnp.asarray(neutral, value.dtype)

    def step(position, subtotal):
        longer = join(subtotal, pieces[position])
        return jnp.where(position < mine, longer, subtotal)

    return lax.fori_loop(0, count - 1, step, subtotal)


def settle_sweep(mixing, settle_rate, inflow):

    def stepper(flux_in, inputs):
        level_mix, level_rate = inputs
        summed = level_mix + flux_in
        return (level_rate / (1.0 + level_rate) * summed, summed / (1.0 + level_rate))

    _, swept = lax.scan(
        stepper, inflow, (jnp.moveaxis(mixing, 2, 0), jnp.moveaxis(settle_rate, 2, 0))
    )
    return jnp.moveaxis(swept, 0, 2)


def add_terms(earlier, later):
    return earlier + later


def on_device(
    particle_mass_fraction,
    meridional_cfl_factor,
    thermal_state_kelvins,
    logarithmic_barometric_span,
    gravitational_fall_kilometres,
    zonal_cfl_factor,
    collision_rate_matrix,
):
    bin_count = particle_mass_fraction.shape[0]
    stacked = jnp.concatenate([particle_mass_fraction, meridional_cfl_factor[None]], 0)
    padded = extended_2(stacked, (("lat", 1),), 1, False)
    rows_below = padded[:bin_count, :-2]
    rows_above = padded[:bin_count, 2:]
    courant_above = padded[bin_count, 2:]
    south_flux = (
        jnp.maximum(meridional_cfl_factor, 0.0) * rows_below
        + jnp.minimum(meridional_cfl_factor, 0.0) * particle_mass_fraction
    )
    north_flux = (
        jnp.maximum(courant_above, 0.0) * particle_mass_fraction
        + jnp.minimum(courant_above, 0.0) * rows_above
    )
    advected = particle_mass_fraction + south_flux - north_flux
    vertical_span_height = (
        specific_air_factor * thermal_state_kelvins * logarithmic_barometric_span[None, :, None]
    )
    column_total = jnp.sum(vertical_span_height, axis=1)
    incoming = prefix(column_total, "lev", add_terms, jnp.zeros_like(column_total))
    height = (
        incoming[:, None, :]
        + jnp.cumsum(vertical_span_height[:, ::-1], axis=1)[:, ::-1]
        - 0.5 * vertical_span_height
    )
    density = jnp.exp(-height / scale_height)
    packed = jnp.concatenate([advected, vertical_span_height[None], density[None]], 0)
    columns = lax.all_to_all(packed, "lev", split_axis=3, concat_axis=2, tiled=True)
    col_thick = columns[bin_count]
    col_density = columns[bin_count + 1]
    settle_rate = gravitational_fall_kilometres[:, None, None, None] / col_thick[None]
    inflow = jnp.zeros((bin_count, columns.shape[1], columns.shape[3]), jnp.float32)
    settled = settle_sweep(columns[:bin_count], settle_rate, inflow)
    extended = extended_2(
        jnp.concatenate([settled, zonal_cfl_factor[None]], 0), (("lev", 3),), 1, True
    )
    west_mix = extended[:bin_count, :, :, :-2]
    east_mix = extended[:bin_count, :, :, 2:]
    courant_east = extended[bin_count, :, :, 2:]
    west_flux = (
        jnp.maximum(zonal_cfl_factor, 0.0) * west_mix + jnp.minimum(zonal_cfl_factor, 0.0) * settled
    )
    east_flux = jnp.maximum(courant_east, 0.0) * settled + jnp.minimum(courant_east, 0.0) * east_mix
    moved = settled + west_flux - east_flux
    merging = jnp.tril(collision_rate_matrix, -1) - jnp.triu(collision_rate_matrix, 1)
    coag_rate = jnp.einsum("bc,clkx->blkx", merging, moved, precision=lax.Precision.HIGHEST)
    return (moved + col_density * moved * coag_rate, height)


def solution(mesh):
    in_specs = (
        P(None, "lat", "lev", None),
        P("lat", "lev", None),
        P("lat", "lev", None),
        P("lev"),
        P(),
        P("lat", None, "lev"),
        P(),
    )
    out_specs = (P(None, "lat", None, "lev"), P("lat", "lev", None))
    return jax.shard_map(
        on_device, mesh=mesh, in_specs=in_specs, out_specs=out_specs, check_vma=False
    )
```

profile of v0, /device:TPU:0, one launch (start us, length us, event | category | flops | bytes accessed | tf_op | source)
XLA Modules:
  0.0 57.4 jit_solution(17528665692314259171)
XLA Ops:
  0.6 0.0 copy-start
  0.6 1.0 %pad_maximum_fusion.11 = (f32[21,1,2,360]{3,2,1,0:T(2,128)S(1)}, f32[21,1,2,360]{3,2,1,0:T(2,128)S(1)}) fusion(f32[1,8,2,360]{3,2,1,0:T(2,128)} %bitcast.67, f32[20,8,2,360]{3,2,1,0:T(2,128)} %param.11), kind=kLoop, calls=%fused_computation.41 | loop fusion | flops 30240 | bytes 604800 | tf_op jit(solution)/shard_map/slice | solution.py:15
  1.7 1.3 %collective-permute-start.1 = (f32[21,1,2,360]{3,2,1,0:T(2,128)S(1)}, f32[21,1,2,360]{3,2,1,0:T(2,128)S(1)}, u32[]{:S(2)}, u32[]{:S(2)}) collective-permute-start(f32[21,1,2,360]{3,2,1,0:T(2,128)S(1)} %get-tuple-element.233), channel_id=1, source_target_pairs={{4,0},{8,4},{12,8},{16,12},{20,16},{24,20},{28,24},{5,1},{9,5},{13... | collective-permute-start | bytes 181448 | tf_op jit(solution)/shard_map/ppermute | solution.py:18
  3.0 5.5 %collective-permute-start = (f32[21,1,2,360]{3,2,1,0:T(2,128)S(1)}, f32[21,1,2,360]{3,2,1,0:T(2,128)S(1)}, u32[]{:S(2)}, u32[]{:S(2)}) collective-permute-start(f32[21,1,2,360]{3,2,1,0:T(2,128)S(1)} %get-tuple-element.232), channel_id=1, source_target_pairs={{0,4},{4,8},{8,12},{12,16},{16,20},{20,24},{24,28},{1,5},{5,9},{9,... | collective-permute-start | bytes 181448 | tf_op jit(solution)/shard_map/ppermute | solution.py:17
  8.4 0.8 %broadcast_maximum_fusion.2 = (f32[8,2,360]{2,1,0:T(2,128)S(1)}, f32[8,2,360]{2,1,0:T(2,128)S(1)}) fusion(f32[8,2,360]{2,1,0:T(2,128)} %param.12), kind=kLoop, calls=%fused_computation.60 | loop fusion | flops 11520 | bytes 69120 | tf_op jit(solution)/shard_map/max | solution.py:70
  9.2 0.7 %broadcast_multiply_fusion = f32[2]{0:T(128)S(1)} fusion(f32[2]{0:T(128)} %param.14), kind=kLoop, calls=%fused_computation.64 | loop fusion | flops 2 | bytes 16 | tf_op jit(solution)/shard_map/mul | solution.py:79
  9.9 0.8 %fusion.29 = (f32[8,360]{1,0:T(8,128)S(1)}, f32[8,2,360]{2,0,1:T(8,128)S(1)}) fusion(f32[2]{0:T(128)S(1)} %broadcast_multiply_fusion, f32[8,2,360]{2,1,0:T(2,128)} %param.13), kind=kLoop, calls=%fused_computation.67 | loop fusion | flops 8640 | bytes 57608 | tf_op jit(solution)/shard_map/reduce_sum | solution.py:81
  10.7 0.1 fusion.31
  10.8 5.3 %all-gather = f32[32,360]{1,0:T(8,128)S(1)} all-gather(f32[8,360]{1,0:T(8,128)S(1)} %get-tuple-element.224), channel_id=2, replica_groups=mesh['lat'=8,'lev'=4] {'lev'}, dimensions={0}, use_global_device_ids=true | all-gather | bytes 57600 | tf_op jit(solution)/shard_map/all_gather | solution.py:25
  16.1 0.1 while.27
  16.2 0.6 %exponential_bitcast_fusion = (f32[1,8,2,360]{3,1,2,0:T(8,128)S(1)}, f32[8,2,360]{2,0,1:T(8,128)}) fusion(f32[8,2,360]{2,0,1:T(8,128)S(1)} %get-tuple-element.225, f32[8,2,360]{2,0,1:T(8,128)S(1)} %fusion.31, f32[8,360]{1,0:T(8,128)S(1)} %get-tuple-element.108), kind=kLoop, calls=%fused_computation.45 | loop fusion | flops 28800 | bytes 103680 | tf_op jit(solution)/shard_map/broadcast_in_dim | solution.py:89
  16.8 0.0 collective-permute-done.1
  16.8 0.8 %maximum_bitcast_fusion = (f32[8,2,360]{2,1,0:T(2,128)S(1)}, f32[1,8,2,360]{3,2,1,0:T(2,128)S(1)}) fusion(f32[21,1,2,360]{3,2,1,0:T(2,128)S(1)} %collective-permute-done.1, f32[1,8,2,360]{3,2,1,0:T(2,128)} %bitcast.68, f32[20,8,2,360]{3,2,1,0:T(2,128)} %param.11), kind=kLoop, calls=%fused_computation.48 | loop fusion | flops 17280 | bytes 590400 | tf_op jit(solution)/shard_map/mul | solution.py:74
  17.7 0.0 collective-permute-done
  17.7 1.7 %pad_maximum_fusion.8 = (f32[20,8,2,360]{3,2,1,0:T(2,128)S(1)}, f32[20,8,2,360]{3,2,1,0:T(2,128)S(1)}) fusion(f32[21,1,2,360]{3,2,1,0:T(2,128)S(1)} %collective-permute-done, f32[1,8,2,360]{3,2,1,0:T(2,128)} %bitcast.69, f32[20,8,2,360]{3,2,1,0:T(2,128)} %param.11, f32[21,1,2,360]{3,2,1,0:T(2,128)S(1)} %collective-permute-done.1), kind=kLoop, calls=%fused_computation.27 | loop fusion | flops 460800 | bytes 1526400 | tf_op jit(solution)/shard_map/concatenate | solution.py:19
  19.4 0.1 fusion.14
  19.6 1.3 %copy.255 = f32[22,8,2,360]{0,1,2,3:T(8,128)S(1)} copy(f32[22,8,2,360]{3,1,2,0:T(8,128)S(1)} %pad_maximum_fusion.5) | data formatting | bytes 1013760 | tf_op jit(solution)/shard_map/concatenate | solution.py:89
  20.9 0.0 copy-start.2
  20.9 3.7 %reshape.18 = f32[4,1,31680]{2,1,0:T(1,128)} reshape(f32[360,2,8,22]{3,2,1,0:T(8,128)S(1)} %bitcast.60) | data formatting | bytes 1013760
  24.6 3.5 %all-to-all-start = ((f32[4,1,31680]{2,1,0:T(1,128)}), f32[4,1,31680]{2,1,0:T(1,128)S(1)}, u32[]{:S(2)}, u32[]{:S(2)}) async-start(f32[4,1,31680]{2,1,0:T(1,128)} %reshape.18), calls=%async_computation | async-start | bytes 1015808 | tf_op jit(solution)/shard_map/all_to_all | solution.py:90
  28.1 0.6 %broadcast_maximum_fusion.1 = (f32[8,8,90]{2,1,0:T(8,128)}, f32[8,8,90]{2,1,0:T(8,128)}) fusion(f32[8,8,90]{2,1,0:T(8,128)S(1)} %copy-done.2), kind=kLoop, calls=%fused_computation.52 | loop fusion | flops 11520 | bytes 69120 | tf_op jit(solution)/shard_map/max | solution.py:103
  28.7 8.1 %all-to-all-done = f32[4,1,31680]{2,1,0:T(1,128)S(1)} async-done(((f32[4,1,31680]{2,1,0:T(1,128)}), f32[4,1,31680]{2,1,0:T(1,128)S(1)}, u32[]{:S(2)}, u32[]{:S(2)}) %all-to-all-start) | async-done | bytes 506912 | tf_op jit(solution)/shard_map/all_to_all | solution.py:90
  36.8 0.6 %broadcast.65 = f32[]{:T(128)} broadcast(f32[]{:T(128)} %constant.131), dimensions={} | broadcast | bytes 8 | tf_op jit(solution)/shard_map/all_to_all | solution.py:90
  37.4 2.2 %reduce = f32[4,31680]{1,0:T(4,128)S(1)} reduce(f32[4,1,31680]{2,1,0:T(1,128)S(1)} %all-to-all-done, f32[]{:T(128)} %broadcast.65), dimensions={1}, to_apply=%all_to_all.11.reduce_sub_computation | reduce | bytes 1013764 | tf_op jit(solution)/shard_map/all_to_all | solution.py:90
  39.6 3.5 %reshape.19 = f32[360,2,8,22]{3,2,1,0:T(8,128)S(1)} reshape(f32[4,31680]{1,0:T(4,128)S(1)} %reduce) | data formatting | bytes 1013760
  43.1 0.0 copy-start.7
  43.1 2.2 %copy.270 = f32[22,8,2,4,90]{4,3,1,2,0:T(4,128)} copy(f32[22,8,2,4,90]{0,1,2,4,3:T(8,128)S(1)} %bitcast.59) | data formatting | bytes 1013760 | tf_op jit(solution)/shard_map/all_to_all | solution.py:90
  45.3 0.8 %fusion.30 = (f32[1,8,4,2,90]{4,2,1,3,0:T(4,128)S(1)}, f32[1,8,4,2,90]{4,2,1,3,0:T(4,128)S(1)}) fusion(f32[22,8,4,2,90]{4,2,1,3,0:T(4,128)} %bitcast.65), kind=kLoop, calls=%fused_computation.68 | loop fusion | bytes 92160 | tf_op jit(solution)/shard_map/slice | solution.py:92
  46.1 1.1 %slice.65 = f32[20,8,4,2,90]{4,2,1,3,0:T(4,128)S(1)} slice(f32[22,8,4,2,90]{4,2,1,3,0:T(4,128)} %bitcast.66), slice={[0:20], [0:8], [0:4], [0:2], [0:90]} | slice | bytes 921600 | tf_op jit(solution)/shard_map/slice | solution.py:95
  47.3 0.0 copy-start.3
  47.4 0.1 broadcast_divide_fusion
  47.5 0.8 %while.28 = (s32[]{:T(128)}, f32[20,8,90]{2,1,0:T(8,128)S(1)}, f32[8,20,8,90]{3,2,1,0:T(8,128)S(1)}, f32[8,20,8,90]{3,2,1,0:T(8,128)S(1)}, f32[8,20,8,90]{3,2,1,0:T(8,128)S(1)}, /*index=5*/s32[]{:T(128)}, s32[]{:T(128)}) while((s32[]{:T(128)}, f32[20,8,90]{2,1,0:T(8,128)S(1)}, f32[8,20,8,90]{3,2,1,0:T(8,128)S(1)}, ...), condition=%wide.region_5.6_spmd.clone, body=%wide.region_4.5_spmd.clone.sunk | while | flops 129603 | bytes 558176 | solution.py:44
  48.3 0.0 copy-start.4
  48.3 0.1 copy.291
  48.5 0.4 slice_maximum_fusion
  48.9 0.0 copy-start.8
  48.9 0.5 copy.263
  49.3 0.0 collective-permute-start.3
  49.4 0.6 %copy.268 = f32[8,2,360]{2,1,0:T(2,128)} copy(f32[8,2,360]{2,0,1:T(8,128)S(1)} %copy-done.4) | data formatting | bytes 46080
  50.0 0.5 copy.261
  50.5 0.7 %collective-permute-start.2 = (f32[21,8,8,1]{0,2,3,1:T(8,128)S(1)}, f32[21,8,8,1]{0,2,3,1:T(8,128)S(1)}, u32[]{:S(2)}, u32[]{:S(2)}) collective-permute-start(f32[21,8,8,1]{0,2,3,1:T(8,128)S(1)} %copy.261), channel_id=1, source_target_pairs={{0,1},{1,2},{2,3},{3,0},{4,5},{5,6},{6,7},{7,4},{8,9},{9,10},{10,1... | collective-permute-start | bytes 16136 | tf_op jit(solution)/shard_map/ppermute | solution.py:17
  51.2 0.0 collective-permute-done.3
  51.2 0.5 copy.264
  51.7 0.3 broadcast_maximum_fusion
  52.0 2.0 %collective-permute-done.2 = f32[21,8,8,1]{0,2,3,1:T(8,128)S(1)} collective-permute-done((f32[21,8,8,1]{0,2,3,1:T(8,128)S(1)}, f32[21,8,8,1]{0,2,3,1:T(8,128)S(1)}, u32[]{:S(2)}, u32[]{:S(2)}) %collective-permute-start.2) | collective-permute-done | bytes 5408 | tf_op jit(solution)/shard_map/ppermute | solution.py:17
  54.1 0.5 copy.262
  54.6 1.9 %fusion.3 = f32[20,8,8,90]{3,0,2,1:T(8,128)S(1)} fusion(f32[21,8,8,1]{3,0,2,1:T(8,128)S(1)} %copy.264, f32[1,8,8,90]{3,0,2,1:T(1,128)S(1)} %bitcast.73, f32[20,8,8,90]{3,0,2,1:T(8,128)S(1)} %bitcast.63, f32[21,8,8,1]{3,0,2,1:T(8,128)S(1)} %copy.262, f32[8,8,90]{2,1,0:T(8,128)S(1)} %copy.266, f32[8,8,90]{2,1,0:T(8,128)S(1)} %bitcast.78, ...), kind=kOutput, calls=%fused_computation.8 | convolution fusion | flops 30760400 | bytes 1072272 | tf_op jit(solution)/shard_map/bc,clkx->blkx/dot_general | solution.py:108
  56.5 1.0 %copy.267 = f32[20,8,8,90]{3,2,1,0:T(8,128)} copy(f32[20,8,8,90]{3,0,2,1:T(8,128)S(1)} %fusion.3) | data formatting | bytes 921600
  (48 shorter events, 0.8 us)
Async XLA Ops:
  0.6 18.8 %copy-start = (f32[20,8,2,360]{3,2,1,0:T(2,128)S(1)}, f32[20,8,2,360]{3,2,1,0:T(2,128)}, u32[]{:S(2)}) copy-start(f32[20,8,2,360]{3,2,1,0:T(2,128)} %param.11) | copy-start | bytes 1382404
  1.7 15.2 %collective-permute-start.1 = (f32[21,1,2,360]{3,2,1,0:T(2,128)S(1)}, f32[21,1,2,360]{3,2,1,0:T(2,128)S(1)}, u32[]{:S(2)}, u32[]{:S(2)}) collective-permute-start(f32[21,1,2,360]{3,2,1,0:T(2,128)S(1)} %get-tuple-element.233), channel_id=1, source_target_pairs={{4,0},{8,4},{12,8},{16,12},{20,16},{24,20},{28,24},{5,1},{9,5},{13... | collective-permute-start | bytes 181448 | tf_op jit(solution)/shard_map/ppermute | solution.py:18
  3.0 14.7 %collective-permute-start = (f32[21,1,2,360]{3,2,1,0:T(2,128)S(1)}, f32[21,1,2,360]{3,2,1,0:T(2,128)S(1)}, u32[]{:S(2)}, u32[]{:S(2)}) collective-permute-start(f32[21,1,2,360]{3,2,1,0:T(2,128)S(1)} %get-tuple-element.232), channel_id=1, source_target_pairs={{0,4},{4,8},{8,12},{12,16},{16,20},{20,24},{24,28},{1,5},{5,9},{9,... | collective-permute-start | bytes 181448 | tf_op jit(solution)/shard_map/ppermute | solution.py:17
  20.9 7.2 %copy-start.2 = (f32[8,8,90]{2,1,0:T(8,128)S(1)}, f32[8,8,90]{2,1,0:T(8,128)}, u32[]{:S(2)}) copy-start(f32[8,8,90]{2,1,0:T(8,128)} %param.16) | copy-start | bytes 69124
  24.6 12.3 %all-to-all-start = ((f32[4,1,31680]{2,1,0:T(1,128)}), f32[4,1,31680]{2,1,0:T(1,128)S(1)}, u32[]{:S(2)}, u32[]{:S(2)}) async-start(f32[4,1,31680]{2,1,0:T(1,128)} %reshape.18), calls=%async_computation | async-start | bytes 1015808 | tf_op jit(solution)/shard_map/all_to_all | solution.py:90
  43.1 4.3 %copy-start.7 = (f32[20]{0:T(128)S(1)}, f32[20]{0:T(128)}, u32[]{:S(2)}) copy-start(f32[20]{0:T(128)} %param.15) | copy-start | bytes 244
  45.3 2.2 %copy-start.1 = (f32[8,20,8,90]{3,2,1,0:T(8,128)S(1)}, f32[8,20,8,90]{3,2,1,0:T(8,128)}, u32[]{:S(2)}) copy-start(f32[8,20,8,90]{3,2,1,0:T(8,128)} %custom-call.2) | copy-start | bytes 1382404
  47.3 1.1 %copy-start.3 = (f32[8,8,90]{2,1,0:T(8,128)S(1)}, f32[8,8,90]{2,1,0:T(8,128)}, u32[]{:S(2)}) copy-start(f32[8,8,90]{2,1,0:T(8,128)} %param.16) | copy-start | bytes 69124
  48.3 1.1 %copy-start.4 = (f32[8,2,360]{2,0,1:T(8,128)S(1)}, f32[8,2,360]{2,0,1:T(8,128)}, u32[]{:S(2)}) copy-start(f32[8,2,360]{2,0,1:T(8,128)} %get-tuple-element.223) | copy-start | bytes 69124
  48.8 5.7 %copy-start.5 = (f32[8,8,90]{2,1,0:T(8,128)S(1)}, f32[8,8,90]{2,1,0:T(8,128)}, u32[]{:S(2)}) copy-start(f32[8,8,90]{2,1,0:T(8,128)} %get-tuple-element.234) | copy-start | bytes 69124
  48.8 5.7 %copy-start.6 = (f32[8,8,90]{2,1,0:T(8,128)S(1)}, f32[8,8,90]{2,1,0:T(8,128)}, u32[]{:S(2)}) copy-start(f32[8,8,90]{2,1,0:T(8,128)} %get-tuple-element.235) | copy-start | bytes 69124
  48.9 5.7 %copy-start.8 = (f32[20,20]{1,0:T(8,128)S(1)}, f32[20,20]{1,0:T(8,128)}, u32[]{:S(2)}) copy-start(f32[20,20]{1,0:T(8,128)} %param.17) | copy-start | bytes 4804
  49.3 1.9 %collective-permute-start.3 = (f32[21,8,8,1]{0,2,3,1:T(8,128)S(1)}, f32[21,8,8,1]{0,2,3,1:T(8,128)S(1)}, u32[]{:S(2)}, u32[]{:S(2)}) collective-permute-start(f32[21,8,8,1]{0,2,3,1:T(8,128)S(1)} %copy.263), channel_id=1, source_target_pairs={{1,0},{2,1},{3,2},{0,3},{5,4},{6,5},{7,6},{4,7},{9,8},{10,9},{11,1... | collective-permute-start | bytes 16136 | tf_op jit(solution)/shard_map/ppermute | solution.py:18
  50.5 3.5 %collective-permute-start.2 = (f32[21,8,8,1]{0,2,3,1:T(8,128)S(1)}, f32[21,8,8,1]{0,2,3,1:T(8,128)S(1)}, u32[]{:S(2)}, u32[]{:S(2)}) collective-permute-start(f32[21,8,8,1]{0,2,3,1:T(8,128)S(1)} %copy.261), channel_id=1, source_target_pairs={{0,1},{1,2},{2,3},{3,0},{4,5},{5,6},{6,7},{7,4},{8,9},{9,10},{10,1... | collective-permute-start | bytes 16136 | tf_op jit(solution)/shard_map/ppermute | solution.py:17
where the time goes:
time: 57.9 us; the launch traced here: 57.4 us
  local copies, waits for them, and re-layouts  17 us (29%)
  starting transfers between devices  11 us (19%)
  other arithmetic  10.8 us (19%)
  waiting for transfers between devices  10.1 us (17%)
  blocking collectives  5.29 us (9%)
  matrix products  1.89 us (3%)
  between operations  1.01 us (2%)
    unnamed x22, local copies, waits for them, and re-layouts  8.74 us
    all_to_all x1, waiting for transfers between devices, on_device(): lax.all_to_all(packed, 'lev', split_axis=3, concat_axis=2, tiled=True)  8.13 us
    ppermute x2, starting transfers between devices, extended_2(): before = lax.ppermute(last, axis, up)  6.16 us
    all_gather x1, blocking collectives, prefix(): pieces = lax.all_gather(value, axis)  5.29 us
    all_to_all x1, starting transfers between devices, on_device(): lax.all_to_all(packed, 'lev', split_axis=3, concat_axis=2, tiled=True)  3.47 us
    all_to_all x2, local copies, waits for them, and re-layouts, on_device(): lax.all_to_all(packed, 'lev', split_axis=3, concat_axis=2, tiled=True)  2.8 us
    all_to_all x1, other arithmetic, on_device(): lax.all_to_all(packed, 'lev', split_axis=3, concat_axis=2, tiled=True)  2.16 us
    ppermute x2, waiting for transfers between devices, extended_2(): before = lax.ppermute(last, axis, up)  2.01 us
  transfers between devices with their start and end apart: 5, of which 2 were waited for; matrix products, arithmetic and copies ran while one was open for 11% of the time, Pallas kernels for 0%

commit v1 on v0

--- a/solution.py
+++ b/solution.py
@@ -87,7 +87,9 @@
     )
     density = jnp.exp(-height / scale_height)
     packed = jnp.concatenate([advected, vertical_span_height[None], density[None]], 0)
-    columns = lax.all_to_all(packed, "lev", split_axis=3, concat_axis=2, tiled=True)
+    parts = jnp.split(packed, lax.axis_size("lev"), axis=3)
+    incoming_2 = lax.all_to_all(jnp.stack(parts), "lev", 0, 0)
+    columns = jnp.concatenate(incoming_2, axis=2)
     col_thick = columns[bin_count]
     col_density = columns[bin_count + 1]
     settle_rate = gravitational_fall_kilometres[:, None, None, None] / col_thick[None]

time: 57.9 us -> 42.9 us (0.74)
  the two profiles are of different devices: /device:TPU:0 before, /device:TPU:16 now
where the time goes in v1:
time: 42.9 us; the launch traced here: 42.4 us
  waiting for transfers between devices  12.9 us (30%)
  starting transfers between devices  10.9 us (25%)
  local copies, waits for them, and re-layouts  7.26 us (17%)
  blocking collectives  5.23 us (12%)
  other arithmetic  3 us (7%)
  matrix products  1.88 us (4%)
  between operations  0.95 us (2%)
    all_to_all x1, waiting for transfers between devices, on_device(): incoming_2 = lax.all_to_all(jnp.stack(parts), 'lev', 0, 0)  10.9 us
    all_gather x1, blocking collectives, prefix(): pieces = lax.all_gather(value, axis)  5.23 us
    unnamed x16, local copies, waits for them, and re-layouts  4.74 us
    ppermute x2, starting transfers between devices, extended_2(): before = lax.ppermute(last, axis, up)  3.91 us
    all_to_all x1, starting transfers between devices, on_device(): incoming_2 = lax.all_to_all(jnp.stack(parts), 'lev', 0, 0)  3.62 us
    ppermute x2, starting transfers between devices, extended_2(): after = lax.ppermute(leading, axis, down)  3.37 us
    ppermute x2, waiting for transfers between devices, extended_2(): before = lax.ppermute(last, axis, up)  2.01 us
    dot_general x1, matrix products, on_device(): jnp.einsum('bc,clkx->blkx', merging, moved, precision=lax.Precision.HIGHEST)  1.88 us
  transfers between devices with their start and end apart: 5, of which 2 were waited for; matrix products, arithmetic and copies ran while one was open for 5% of the time, Pallas kernels for 0%

profile of v1, /device:TPU:16, one launch (start us, length us, event | category | flops | bytes accessed | tf_op | source)
XLA Modules:
  0.0 42.4 jit_solution(478763982617535670)
XLA Ops:
  0.6 0.7 %copy.56 = f32[8,2,360]{2,0,1:T(8,128)S(1)} copy(f32[8,2,360]{2,1,0:T(2,128)} %param.12) | data formatting | bytes 46080 | tf_op args[1]
  1.4 1.1 %copy.33 = f32[20,8,2,360]{3,1,2,0:T(8,128)S(1)} copy(f32[20,8,2,360]{3,2,1,0:T(2,128)} %param.11) | data formatting | bytes 921600 | tf_op args[0]
  2.4 0.0 copy-start.1
  2.4 0.1 pad_maximum_fusion.12
  2.5 3.4 %collective-permute-start = (f32[21,1,2,360]{3,1,2,0:T(1,128)S(1)}, f32[21,1,2,360]{3,1,2,0:T(1,128)S(1)}, u32[]{:S(2)}, u32[]{:S(2)}) collective-permute-start(f32[21,1,2,360]{3,1,2,0:T(1,128)S(1)} %get-tuple-element.183), channel_id=1, source_target_pairs={{0,4},{4,8},{8,12},{12,16},{16,20},{20,24},{24,28},{1,5},{5,9},{9,... | collective-permute-start | bytes 181448 | tf_op jit(solution)/shard_map/ppermute | solution.py:17
  5.9 3.3 %collective-permute-start.1 = (f32[21,1,2,360]{3,1,2,0:T(1,128)S(1)}, f32[21,1,2,360]{3,1,2,0:T(1,128)S(1)}, u32[]{:S(2)}, u32[]{:S(2)}) collective-permute-start(f32[21,1,2,360]{3,1,2,0:T(1,128)S(1)} %get-tuple-element.184), channel_id=1, source_target_pairs={{4,0},{8,4},{12,8},{16,12},{20,16},{24,20},{28,24},{5,1},{9,5},{13... | collective-permute-start | bytes 181448 | tf_op jit(solution)/shard_map/ppermute | solution.py:18
  9.3 0.0 copy-done.1
  9.3 0.0 copy-start.2
  9.4 0.0 copy-start.5
  9.4 0.6 %copy-done.5 = f32[2]{0:T(128)S(1)} copy-done((f32[2]{0:T(128)S(1)}, f32[2]{0:T(128)}, u32[]{:S(2)}) %copy-start.5) | copy-done | bytes 32
  10.0 0.0 copy-done.2
  10.1 0.1 fusion.31
  10.1 0.1 fusion.33
  10.3 5.2 %all-gather = f32[32,360]{1,0:T(8,128)S(1)} all-gather(f32[8,360]{1,0:T(8,128)S(1)} %get-tuple-element.173), channel_id=2, replica_groups=mesh['lat'=8,'lev'=4] {'lev'}, dimensions={0}, use_global_device_ids=true | all-gather | bytes 57600 | tf_op jit(solution)/shard_map/all_gather | solution.py:25
  15.5 0.1 while.27
  15.6 0.0 collective-permute-done.1
  15.7 0.0 collective-permute-done
  15.7 0.3 fusion.15
  16.1 0.2 slice_bitcast_fusion.3
  16.3 1.0 %pad_maximum_fusion.5 = f32[4,22,8,2,90]{4,2,3,1,0:T(8,128)} fusion(f32[1,22,8,2,90]{4,2,3,1,0:T(8,128)S(1)} %get-tuple-element.180, f32[1,22,8,2,90]{4,2,3,1,0:T(8,128)S(1)} %get-tuple-element.181, f32[1,22,8,2,90]{4,2,3,1,0:T(8,128)S(1)} %get-tuple-element.182, f32[1,22,8,2,90]{4,2,3,1,0:T(8,128)S(1)} %get-tuple-element.179), kind=kLoop, calls=%fused_computation.24 | loop fusion | flops 380160 | bytes 1013760 | tf_op jit(solution)/shard_map/stack | solution.py:91
  17.2 0.0 copy-start
  17.2 3.6 %all-to-all-start = ((f32[4,22,8,2,90]{4,2,3,1,0:T(8,128)}), f32[4,22,8,2,90]{4,2,3,1,0:T(8,128)S(1)}, u32[]{:S(2)}, u32[]{:S(2)}) async-start(f32[4,22,8,2,90]{4,2,3,1,0:T(8,128)} %pad_maximum_fusion.5), calls=%async_computation | async-start | bytes 1441792 | tf_op jit(solution)/shard_map/all_to_all | solution.py:91
  20.9 0.0 copy-done
  20.9 10.9 %all-to-all-done = f32[4,22,8,2,90]{4,2,3,1,0:T(8,128)S(1)} async-done(((f32[4,22,8,2,90]{4,2,3,1,0:T(8,128)}), f32[4,22,8,2,90]{4,2,3,1,0:T(8,128)S(1)}, u32[]{:S(2)}, u32[]{:S(2)}) %all-to-all-start) | async-done | bytes 506912 | tf_op jit(solution)/shard_map/all_to_all | solution.py:91
  31.8 0.1 copy.54
  31.9 0.1 slice.65
  32.0 0.0 copy-start.3
  32.0 0.6 %copy-done.3 = f32[20]{0:T(128)S(1)} copy-done((f32[20]{0:T(128)S(1)}, f32[20]{0:T(128)}, u32[]{:S(2)}) %copy-start.3) | copy-done | bytes 104
  32.6 0.1 broadcast_divide_fusion
  32.7 0.8 %while.28 = (s32[]{:T(128)}, f32[20,8,90]{2,1,0:T(8,128)S(1)}, f32[8,20,8,90]{3,2,1,0:T(8,128)S(1)}, f32[8,20,8,90]{3,2,1,0:T(8,128)S(1)}, f32[8,20,8,90]{3,2,1,0:T(8,128)S(1)}, /*index=5*/s32[]{:T(128)}, s32[]{:T(128)}) while((s32[]{:T(128)}, f32[20,8,90]{2,1,0:T(8,128)S(1)}, f32[8,20,8,90]{3,2,1,0:T(8,128)S(1)}, ...), condition=%wide.region_5.6_spmd.clone, body=%wide.region_4.5_spmd.clone.sunk | while | flops 129603 | bytes 558184 | solution.py:44
  33.5 0.1 copy.53
  33.7 0.4 slice_maximum_fusion
  34.1 0.5 %copy.41 = f32[21,8,8,1]{0,2,3,1:T(8,128)S(1)} copy(f32[21,8,8,1]{3,0,2,1:T(8,128)S(1)} %get-tuple-element.176) | data formatting | bytes 10752 | tf_op jit(solution)/shard_map/slice | solution.py:16
  34.5 0.0 collective-permute-start.3
  34.6 0.6 %copy.45 = f32[8,2,360]{2,1,0:T(2,128)} copy(f32[8,2,360]{2,0,1:T(8,128)S(1)} %get-tuple-element.172) | data formatting | bytes 46080
  35.2 0.5 %copy.39 = f32[21,8,8,1]{0,2,3,1:T(8,128)S(1)} copy(f32[21,8,8,1]{3,0,2,1:T(8,128)S(1)} %get-tuple-element.175) | data formatting | bytes 10752 | tf_op jit(solution)/shard_map/slice | solution.py:15
  35.7 0.5 %collective-permute-start.2 = (f32[21,8,8,1]{0,2,3,1:T(8,128)S(1)}, f32[21,8,8,1]{0,2,3,1:T(8,128)S(1)}, u32[]{:S(2)}, u32[]{:S(2)}) collective-permute-start(f32[21,8,8,1]{0,2,3,1:T(8,128)S(1)} %copy.39), channel_id=1, source_target_pairs={{0,1},{1,2},{2,3},{3,0},{4,5},{5,6},{6,7},{7,4},{8,9},{9,10},{10,1... | collective-permute-start | bytes 16136 | tf_op jit(solution)/shard_map/ppermute | solution.py:17
  36.2 0.0 collective-permute-done.3
  36.2 0.5 %copy.42 = f32[21,8,8,1]{3,0,2,1:T(8,128)S(1)} copy(f32[21,8,8,1]{0,2,3,1:T(8,128)S(1)} %collective-permute-done.3) | data formatting | bytes 10752 | tf_op jit(solution)/shard_map/ppermute | solution.py:18
  36.7 0.3 broadcast_maximum_fusion
  37.0 0.0 copy-start.4
  37.1 2.0 %collective-permute-done.2 = f32[21,8,8,1]{0,2,3,1:T(8,128)S(1)} collective-permute-done((f32[21,8,8,1]{0,2,3,1:T(8,128)S(1)}, f32[21,8,8,1]{0,2,3,1:T(8,128)S(1)}, u32[]{:S(2)}, u32[]{:S(2)}) %collective-permute-start.2) | collective-permute-done | bytes 5408 | tf_op jit(solution)/shard_map/ppermute | solution.py:17
  39.1 0.5 %copy.40 = f32[21,8,8,1]{3,0,2,1:T(8,128)S(1)} copy(f32[21,8,8,1]{0,2,3,1:T(8,128)S(1)} %collective-permute-done.2) | data formatting | bytes 10752 | tf_op jit(solution)/shard_map/ppermute | solution.py:17
  39.6 0.0 copy-done.4
  39.6 1.9 %fusion.3 = f32[20,8,8,90]{3,0,2,1:T(8,128)S(1)} fusion(f32[21,8,8,1]{3,0,2,1:T(8,128)S(1)} %copy.42, f32[1,8,8,90]{3,0,2,1:T(1,128)S(1)} %bitcast.82, f32[20,8,8,90]{3,0,2,1:T(8,128)S(1)} %bitcast.71, f32[21,8,8,1]{3,0,2,1:T(8,128)S(1)} %copy.40, f32[8,8,90]{2,1,0:T(8,128)S(1)} %copy.43, f32[8,8,90]{2,1,0:T(8,128)S(1)} %bitcast.87, ...), kind=kOutput, calls=%fused_computation.8 | convolution fusion | flops 30760400 | bytes 1072272 | tf_op jit(solution)/shard_map/bc,clkx->blkx/dot_general | solution.py:110
  41.5 1.0 %copy.44 = f32[20,8,8,90]{3,2,1,0:T(8,128)} copy(f32[20,8,8,90]{3,0,2,1:T(8,128)S(1)} %fusion.3) | data formatting | bytes 921600
  (38 shorter events, 0.8 us)
Async XLA Ops:
  2.4 6.9 %copy-start.1 = (f32[8,2,360]{2,1,0:T(2,128)S(1)}, f32[8,2,360]{2,1,0:T(2,128)}, u32[]{:S(2)}) copy-start(f32[8,2,360]{2,1,0:T(2,128)} %param.12) | copy-start | bytes 69124
  2.5 13.1 %collective-permute-start = (f32[21,1,2,360]{3,1,2,0:T(1,128)S(1)}, f32[21,1,2,360]{3,1,2,0:T(1,128)S(1)}, u32[]{:S(2)}, u32[]{:S(2)}) collective-permute-start(f32[21,1,2,360]{3,1,2,0:T(1,128)S(1)} %get-tuple-element.183), channel_id=1, source_target_pairs={{0,4},{4,8},{8,12},{12,16},{16,20},{20,24},{24,28},{1,5},{5,9},{9,... | collective-permute-start | bytes 181448 | tf_op jit(solution)/shard_map/ppermute | solution.py:17
  5.9 9.7 %collective-permute-start.1 = (f32[21,1,2,360]{3,1,2,0:T(1,128)S(1)}, f32[21,1,2,360]{3,1,2,0:T(1,128)S(1)}, u32[]{:S(2)}, u32[]{:S(2)}) collective-permute-start(f32[21,1,2,360]{3,1,2,0:T(1,128)S(1)} %get-tuple-element.184), channel_id=1, source_target_pairs={{4,0},{8,4},{12,8},{16,12},{20,16},{24,20},{28,24},{5,1},{9,5},{13... | collective-permute-start | bytes 181448 | tf_op jit(solution)/shard_map/ppermute | solution.py:18
  9.3 0.7 %copy-start.2 = (f32[8,2,360]{2,1,0:T(2,128)S(1)}, f32[8,2,360]{2,1,0:T(2,128)}, u32[]{:S(2)}) copy-start(f32[8,2,360]{2,1,0:T(2,128)} %param.13) | copy-start | bytes 69124
  9.4 0.7 %copy-start.5 = (f32[2]{0:T(128)S(1)}, f32[2]{0:T(128)}, u32[]{:S(2)}) copy-start(f32[2]{0:T(128)} %param.14) | copy-start | bytes 28
  17.2 3.6 %copy-start = (f32[8,8,90]{2,1,0:T(8,128)S(1)}, f32[8,8,90]{2,1,0:T(8,128)}, u32[]{:S(2)}) copy-start(f32[8,8,90]{2,1,0:T(8,128)} %param.16) | copy-start | bytes 69124
  17.2 14.5 %all-to-all-start = ((f32[4,22,8,2,90]{4,2,3,1,0:T(8,128)}), f32[4,22,8,2,90]{4,2,3,1,0:T(8,128)S(1)}, u32[]{:S(2)}, u32[]{:S(2)}) async-start(f32[4,22,8,2,90]{4,2,3,1,0:T(8,128)} %pad_maximum_fusion.5), calls=%async_computation | async-start | bytes 1441792 | tf_op jit(solution)/shard_map/all_to_all | solution.py:91
  32.0 0.7 %copy-start.3 = (f32[20]{0:T(128)S(1)}, f32[20]{0:T(128)}, u32[]{:S(2)}) copy-start(f32[20]{0:T(128)} %param.15) | copy-start | bytes 244
  34.5 1.7 %collective-permute-start.3 = (f32[21,8,8,1]{0,2,3,1:T(8,128)S(1)}, f32[21,8,8,1]{0,2,3,1:T(8,128)S(1)}, u32[]{:S(2)}, u32[]{:S(2)}) collective-permute-start(f32[21,8,8,1]{0,2,3,1:T(8,128)S(1)} %copy.41), channel_id=1, source_target_pairs={{1,0},{2,1},{3,2},{0,3},{5,4},{6,5},{7,6},{4,7},{9,8},{10,9},{11,1... | collective-permute-start | bytes 16136 | tf_op jit(solution)/shard_map/ppermute | solution.py:18
  35.7 3.4 %collective-permute-start.2 = (f32[21,8,8,1]{0,2,3,1:T(8,128)S(1)}, f32[21,8,8,1]{0,2,3,1:T(8,128)S(1)}, u32[]{:S(2)}, u32[]{:S(2)}) collective-permute-start(f32[21,8,8,1]{0,2,3,1:T(8,128)S(1)} %copy.39), channel_id=1, source_target_pairs={{0,1},{1,2},{2,3},{3,0},{4,5},{5,6},{6,7},{7,4},{8,9},{9,10},{10,1... | collective-permute-start | bytes 16136 | tf_op jit(solution)/shard_map/ppermute | solution.py:17
  37.0 2.5 %copy-start.4 = (f32[20,20]{1,0:T(8,128)S(1)}, f32[20,20]{1,0:T(8,128)}, u32[]{:S(2)}) copy-start(f32[20,20]{1,0:T(8,128)} %param.17) | copy-start | bytes 4804
